TPU v7x, 32 devices: a whole 2x2x4 slice. The times are simulated.
32 devices in a mesh: dp: 2 (over x), feat: 16 (over z, y, core).
Axes of the slice: x: 2, y: 2, z: 4, core: 2. Of those that a mesh axis runs over, the one named last changes fastest.
Arguments:
- feature_slab: float32 [1024, 28672], P('dp', 'feat'), may hold values from -200 to 200, as said below
- basis_start: float32 [28672, 256], P('feat'), may hold values from -0.03125 to 0.03125
Outputs:
- basis_out: float32 [28672, 256], P('feat')
Inputs may be any that keep to these rules, and one draw needn't show every extreme that they name: `feature_slab`: Real-valued entries; column scales differ over features and row scales over rows.
All inputs are finite; a program needn't handle non-finite values.
Results may differ from a plain program's by a relative error of at most 0.0015.
Values sent between devices are 32-bit elements; how exact they have to be, the bound alone decides.
A program may use at most 64 MiB of HBM per device.

v0:
```python
import math

import jax
import jax.numpy as jnp
from jax import lax
from jax.sharding import PartitionSpec as P

FF = 28672
NS_STEPS = 5


coef_first = 3.4445
coef_second = -4.775
coef_third = 2.0315


def plain_dot(left, right):
    return jnp.dot(left, right, precision=lax.Precision.HIGHEST, preferred_element_type=jnp.float32)


def inner_dot(left, right):
    return lax.dot_general(
        left,
        right,
        (((0,), (0,)), ((), ())),
        precision=lax.Precision.HIGHEST,
        preferred_element_type=jnp.float32,
    )


def newton_schulz(matrix):
    polar_iter = matrix / jnp.sqrt(jnp.sum(matrix * matrix) + 1e-12)
    for step_index in range(NS_STEPS):
        square_part = plain_dot(polar_iter, polar_iter.T)
        mixed_part = coef_second * square_part + coef_third * plain_dot(square_part, square_part)
        polar_iter = coef_first * polar_iter + plain_dot(mixed_part, polar_iter)
    return polar_iter


def cholesky_inverse(gram_matrix):
    lower_factor = jnp.linalg.cholesky(gram_matrix)
    identity = jnp.eye(gram_matrix.shape[0], dtype=gram_matrix.dtype)
    return jax.scipy.linalg.solve_triangular(lower_factor, identity, lower=True)


def per_device(feature_slab, basis_start):
    basis = basis_start
    groups = lax.axis_size("dp")
    projected = lax.psum(plain_dot(feature_slab, basis), "feat")
    power_image = inner_dot(feature_slab, projected)
    gram_matrix, cross_terms = lax.psum(
        (inner_dot(power_image, power_image), inner_dot(basis, power_image)), "feat"
    )
    inverse = cholesky_inverse(gram_matrix)
    orthonormal = plain_dot(power_image, inverse.T)
    correlation = plain_dot(cross_terms, inverse.T)
    aligned = plain_dot(orthonormal, newton_schulz(correlation.T))
    basis = lax.psum(aligned, "dp") / groups
    return basis * math.sqrt(FF)


def solution(mesh):
    placed = (P("dp", "feat"), P("feat", None))
    return jax.shard_map(
        per_device, mesh=mesh, in_specs=placed, out_specs=P("feat", None), check_vma=False
    )
```

profile of v0, /device:TPU:0, one launch (start us, length us, event | category | flops | bytes accessed | tf_op | source)
XLA Modules:
  0.0 354.2 jit_solution(7056619013082045333)
XLA Ops:
  6.5 1.5 copy-done
  8.0 5.9 %fusion.19 = f32[512,256]{1,0:T(8,128)} fusion(f32[512,1792]{1,0:T(8,128)} %param.2, f32[1792,256]{1,0:T(8,128)S(1)} %copy-done), kind=kOutput, calls=%fused_computation.54 | convolution fusion | flops 2818572288 | bytes 6029312 | tf_op jit(solution)/shard_map/dot_general | solution.py:18
  14.0 92.9 %all-reduce.6.cloned.1.call-done = f32[512,256]{1,0:T(8,128)} async-done(((f32[512,256]{1,0:T(8,128)}), f32[512,256]{1,0:T(8,128)}) %all-reduce.6.cloned.1.call-update) | async-done | bytes 524304 | tf_op jit(solution)/shard_map/psum | solution.py:49
  106.9 5.5 %fusion.20 = f32[256,1792]{1,0:T(8,128)S(1)} fusion(f32[512,256]{1,0:T(8,128)} %all-reduce.6.cloned.1.call-done, f32[512,1792]{1,0:T(8,128)} %param.2), kind=kOutput, calls=%fused_computation.55 | convolution fusion | flops 2818572288 | bytes 6029312 | tf_op jit(solution)/shard_map/dot_general | solution.py:22
  112.4 2.4 convolution_bitcast_fusion
  114.8 2.4 fusion.21
  117.4 90.3 %all-reduce.10.cloned.1.call-done = (f32[256,256]{0,1:T(8,128)}, f32[256,256]{0,1:T(8,128)}) async-done(((f32[256,256]{0,1:T(8,128)}, f32[256,256]{0,1:T(8,128)}), (f32[256,256]{0,1:T(8,128)}, f32[256,256]{0,1:T(8,128)})) %all-reduce.10.cloned.1.call-update) | async-done | bytes 524304 | tf_op jit(solution)/shard_map/psum | solution.py:51
  207.8 1.1 copy.4
  208.8 1.0 fusion.5
  209.8 11.7 %cholesky.50 = f32[128,128]{1,0:T(8,128)S(1)} custom-call(f32[128,128]{1,0:T(8,128)S(1)} %cholesky.118), custom_call_target="Cholesky" | custom-call | tf_op jit(solution)/shard_map/jit(cholesky)/cholesky | solution.py:41
  221.6 9.8 %custom-call.15 = f32[1,128,128]{1,2,0:T(8,128)S(1)} custom-call(f32[1,128,128]{2,1,0:T(8,128)S(1)} %get-tuple-element.28), custom_call_target="InvertDiagBlocksLowerTriangular" | custom-call | tf_op jit(solution)/shard_map/jit(cholesky)/cholesky | solution.py:41
  231.9 11.7 %cholesky.105 = f32[128,128]{1,0:T(8,128)S(1)} custom-call(f32[128,128]{1,0:T(8,128)S(1)} %convolution_subtract_fusion.1), custom_call_target="Cholesky" | custom-call | tf_op jit(solution)/shard_map/jit(cholesky)/cholesky | solution.py:41
  243.7 0.7 compare_reduce_fusion
  245.8 4.1 %while.1 = (s32[]{:T(128)}, f32[256,256]{1,0:T(8,128)S(1)}, s32[2,2]{1,0:T(2,128)S(1)}, f32[2,128,128]{2,1,0:T(8,128)S(1)}, s32[]{:T(128)}) while((s32[]{:T(128)}, f32[256,256]{1,0:T(8,128)S(1)}, s32[2,2]{1,0:T(2,128)S(1)}, f32[2,128,128]{2,1,0:T(8,128)S(1)}, s32[]{:T(128)}) %tuple.24), condition=%wide.while_cond, body=%wide.while_body.sunk | while | flops 2 | bytes 131189 | solution.py:43
  245.8 0.7 fusion.71
  246.4 1.3 bitcast_dynamic-update-slice_fusion.2
  247.8 0.7 fusion.71
  248.5 1.3 bitcast_dynamic-update-slice_fusion.2
  249.8 19.9 %custom-call.16 = f32[2,128,128]{1,2,0:T(8,128)S(1)} custom-call(f32[2,128,128]{2,1,0:T(8,128)S(1)} %get-tuple-element.12), custom_call_target="InvertDiagBlocksLowerTriangular" | custom-call | tf_op jit(solution)/shard_map/jit(_solve_triangular)/triangular_solve | solution.py:43
  270.6 5.8 %fusion.7 = f32[1792,256]{1,0:T(8,128)} fusion(f32[256,1792]{1,0:T(8,128)} %copy-done.1, f32[128,256]{1,0:T(8,128)S(1)} %fusion.12, f32[128,256]{1,0:T(8,128)S(1)} %fusion.8), kind=kOutput, calls=%fused_computation.29 | convolution fusion | flops 1409351680 | bytes 3932160 | tf_op jit(solution)/shard_map/dot_general | solution.py:18
  276.4 1.0 multiply_reduce_fusion
  278.1 0.4 fusion.10
  278.5 0.4 fusion.4
  278.9 0.4 convolution_add_fusion.4
  279.3 0.4 fusion.22
  280.5 0.4 fusion.23
  281.7 0.4 fusion.24
  282.9 0.4 fusion.25
  283.3 0.4 fusion
  284.1 2.8 fusion.26
  286.9 57.9 %all-reduce.8.cloned.1.call-done = f32[1792,256]{1,0:T(8,128)} async-done(((f32[1792,256]{1,0:T(8,128)}), f32[1792,256]{1,0:T(8,128)}) %all-reduce.8.cloned.1.call-update) | async-done | bytes 1835024 | tf_op jit(solution)/shard_map/psum | solution.py:58
  344.8 2.9 broadcast_multiply_fusion
  (36 shorter events, 4.5 us)
Async XLA Ops:
  6.5 1.5 copy-start
  6.5 100.3 %all-reduce.6.cloned.1.call-start = ((), (), s32[]{:S(2)}) async-start(), calls=%async_computation | async-start | bytes 1048576 | tf_op jit(solution)/shard_map/psum | solution.py:49
  13.9 193.8 %all-reduce.10.cloned.1.call-start = ((), (), s32[]{:S(2)}) async-start(), calls=%async_computation.2 | async-start | bytes 1048576 | tf_op jit(solution)/shard_map/psum | solution.py:51
  112.4 2.4 copy-start.1
  117.1 227.7 %all-reduce.8.cloned.1.call-start = ((), (), s32[]{:S(2)}) async-start(), calls=%async_computation.1 | async-start | bytes 3670016 | tf_op jit(solution)/shard_map/psum | solution.py:58
  270.6 5.8 %copy-start.3 = (f32[256,256]{0,1:T(8,128)S(1)}, f32[256,256]{0,1:T(8,128)}, u32[]{:S(2)}) copy-start(f32[256,256]{0,1:T(8,128)} %get-tuple-element.22) | copy-start | bytes 786436
  282.1 2.0 copy-start.2
Sparse Core Ops, SparseCore 0:
  14.0 92.7 all-reduce.5
  117.3 90.4 all-reduce.9
  287.1 57.7 all-reduce.7
where the time goes:
time: 355 us; the launch traced here: 354 us
  waiting for transfers between devices  241 us (68%)
  other arithmetic  57.9 us (16%)
  matrix products  32.9 us (9%)
  between operations  15.3 us (4%)
  local copies, waits for them, and re-layouts  6.71 us (2%)
    psum x1, waiting for transfers between devices, per_device(): projected = lax.psum(plain_dot(feature_slab, basis), 'feat')  92.9 us
    psum x1, waiting for transfers between devices, per_device(): lax.psum((inner_dot(power_image, power_image), inner_dot(basis, power_ima...  90.3 us
    psum x1, waiting for transfers between devices, per_device(): basis = lax.psum(aligned, 'dp') / groups  57.9 us
    another operation x6, other arithmetic, cholesky_inverse(): lower_factor = jnp.linalg.cholesky(gram_matrix)  34 us
    dot_general x19, matrix products, plain_dot(): jnp.dot(left, right, precision=lax.Precision.HIGHEST, preferred_element_t...  21.4 us
    another operation x3, other arithmetic, cholesky_inverse(): return jax.scipy.linalg.solve_triangular(lower_factor, identity, lower=True)  19.9 us
    dot_general x3, matrix products, inner_dot(): lax.dot_general(left, right, (((0,), (0,)), ((), ())), precision=lax.Prec...  10.2 us
  transfers between devices with their start and end apart: 3, of which 3 were waited for; matrix products, arithmetic and copies ran while one was open for 0% of the time, Pallas kernels for 0%

commit v1 on v0

v1 whole, which is shorter than its diff:
```python
import functools
import math

import jax
import jax.numpy as jnp
from jax import lax
from jax.experimental import pallas as pl
from jax.experimental.pallas import tpu as pltpu
from jax.sharding import PartitionSpec as P

NS_STEPS = 5

coef_first = 3.4445
coef_second = -4.775
coef_third = 2.0315

MESH = pl.DeviceIdType.MESH
NN = (((1,), (0,)), ((), ()))
NT = (((1,), (1,)), ((), ()))
TN = (((0,), (0,)), ((), ()))


def dot6(left, right, dims=NN):
    return lax.dot_general(
        left, right, dims, precision=lax.Precision.HIGHEST, preferred_element_type=jnp.float32
    )


def halves(value):
    high = value.astype(jnp.bfloat16)
    low = (value - high.astype(jnp.float32)).astype(jnp.bfloat16)
    return high, low


def dot3(left, right, dims=NN):
    def dot(a, b):
        return lax.dot_general(a, b, dims, preferred_element_type=jnp.float32)

    return dot(left[0], right[0]) + (dot(left[0], right[1]) + dot(left[1], right[0]))


def radices(count):
    found = []
    while count > 1:
        radix = 2 if len(found) < 2 else 4
        if count % radix:
            radix = 2 if count % 2 == 0 else count
        found.append(radix)
        count //= radix
    return found


def stages_of(count):
    stride, out = 1, []
    for radix in radices(count):
        out.append((radix, stride))
        stride *= radix
    return out


def inverse_factor(block):
    size = block.shape[0]
    lane = lax.broadcasted_iota(jnp.int32, (1, size), 1)
    step = size // 4
    done = []
    top = 0
    for k in range(size):
        if k and k % step == 0:
            done.append(block[:step])
            block = block[step:]
            top = k
        row_id = lax.broadcasted_iota(jnp.int32, block.shape, 0) + top
        lane_id = lax.broadcasted_iota(jnp.int32, block.shape, 1)
        row = block[k - top : k - top + 1, :]
        scale = 1.0 / row[:, k : k + 1]
        row = jnp.where(lane == k, 1.0, row) * scale
        column = jnp.where(row_id[:, :1] > k, block[:, k : k + 1], 0.0)
        block = jnp.where((lane_id == k) & (row_id > k), 0.0, block) - column * row
    done.append(block)
    block = jnp.concatenate(done, axis=0)
    row_id = lax.broadcasted_iota(jnp.int32, block.shape, 0)
    lane_id = lax.broadcasted_iota(jnp.int32, block.shape, 1)
    pivots = jnp.sum(jnp.where(row_id == lane_id, block, 0.0), axis=1, keepdims=True)
    unit = jnp.where(row_id > lane_id, block, jnp.where(row_id == lane_id, 1.0, 0.0))
    return unit * (1.0 / jnp.sqrt(pivots))


def all_reduce(buf, total, slots, sems, stages, me):
    send1, recv1, send2, recv2 = sems
    rows = buf.shape[0]
    at, length, sem = 0, rows, 0
    places = []
    for (radix, stride), slot in zip(stages, slots):
        digit = lax.rem(lax.div(me, stride), radix)
        length //= radix
        copies = []
        for o in range(1, radix):
            other = lax.rem(digit + o, radix)
            copy = pltpu.make_async_remote_copy(
                src_ref=buf.at[pl.ds(pl.multiple_of(at + other * length, 8), length)],
                dst_ref=slot.at[o - 1],
                send_sem=send1.at[sem],
                recv_sem=recv1.at[sem],
                device_id={"feat": me + (other - digit) * stride},
                device_id_type=MESH,
            )
            copy.start()
            copies.append(copy)
            sem += 1
        at = pl.multiple_of(at + digit * length, 8)
        places.append((radix, stride, digit, at, length))
        for copy in copies:
            copy.wait()
        mine = buf[pl.ds(at, length)]
        for o in range(1, radix):
            mine = mine + slot[o - 1]
        if stride * radix == math.prod(r for r, _ in stages):
            total[pl.ds(at, length)] = mine
        else:
            buf[pl.ds(at, length)] = mine
    sem = 0
    for radix, stride, digit, at, length in reversed(places):
        copies = []
        for o in range(1, radix):
            other = lax.rem(digit + o, radix)
            copy = pltpu.make_async_remote_copy(
                src_ref=total.at[pl.ds(at, length)],
                dst_ref=total.at[pl.ds(at, length)],
                send_sem=send2.at[sem],
                recv_sem=recv2.at[sem],
                device_id={"feat": me + (other - digit) * stride},
                device_id_type=MESH,
            )
            copy.start()
            copies.append(copy)
            sem += 1
        for copy in copies:
            copy.wait()


def kernel(cfg, a_ref, b_ref, o_ref, *refs):
    stages, groups, chunks, width, scale_out = cfg
    n = len(stages)
    s_buf, proj, g_buf, g_sum, pit, pit_in, m_buf, m_in = refs[:8]
    s_slots, g_slots = refs[8 : 8 + n], refs[8 + n : 8 + 2 * n]
    s_sems, g_sems = refs[8 + 2 * n : 12 + 2 * n], refs[12 + 2 * n : 16 + 2 * n]
    p_send, p_recv, m_send, m_recv = refs[16 + 2 * n : 20 + 2 * n]
    rank = b_ref.shape[1]
    half = rank // 2
    me = lax.axis_index("feat")
    group = lax.axis_index("dp")

    barrier = pltpu.get_barrier_semaphore()
    count = 0
    for radix, stride in stages:
        digit = lax.rem(lax.div(me, stride), radix)
        for o in range(1, radix):
            other = lax.rem(digit + o, radix)
            pl.semaphore_signal(
                barrier, inc=1, device_id={"feat": me + (other - digit) * stride}, device_id_type=MESH
            )
            count += 1
    for o in range(1, groups):
        pl.semaphore_signal(
            barrier, inc=1, device_id={"dp": lax.rem(group + o, groups)}, device_id_type=MESH
        )
        count += 1

    def columns(c):
        return pl.ds(pl.multiple_of(c * width, width), width) if chunks > 1 else pl.ds(0, width)

    s_buf[...] = jnp.zeros_like(s_buf)

    @pl.loop(0, chunks)
    def _(c):
        s_buf[...] += dot3(halves(a_ref[:, columns(c)]), halves(b_ref[columns(c), :]))

    pl.semaphore_wait(barrier, count)
    all_reduce(s_buf, proj, s_slots, s_sems, stages, me)

    def exchange(c, o):
        return pltpu.make_async_remote_copy(
            src_ref=pit.at[c],
            dst_ref=pit_in.at[o - 1, c],
            send_sem=p_send.at[o - 1, c],
            recv_sem=p_recv.at[o - 1, c],
            device_id={"dp": lax.rem(group + o, groups)},
            device_id_type=MESH,
        )

    projected = halves(proj[...].T)
    m_buf[...] = jnp.zeros_like(m_buf)

    @pl.loop(0, chunks)
    def _(c):
        image = dot3(projected, halves(a_ref[:, columns(c)]))
        pit[c] = image
        for o in range(1, groups):
            exchange(c, o).start()
        pair = halves(image)
        m_buf[...] += dot3(pair, pair, NT)

    g_buf[0:half] = m_buf[:half, :half]
    g_buf[half : 2 * half] = m_buf[:half, half:]
    g_buf[2 * half : 3 * half] = m_buf[half:, half:]
    if g_buf.shape[0] > 3 * half:
        g_buf[3 * half :] = jnp.zeros_like(g_buf[3 * half :])
    all_reduce(g_buf, g_sum, g_slots, g_sems, stages, me)

    first = inverse_factor(g_sum[0:half])
    upper = dot6(first, g_sum[half : 2 * half])
    last = inverse_factor(g_sum[2 * half : 3 * half] - dot6(upper, upper, TN))
    low = -dot6(last, dot6(upper, first, TN))
    inverse = jnp.concatenate(
        [
            jnp.concatenate([first, jnp.zeros_like(first)], axis=1),
            jnp.concatenate([low, last], axis=1),
        ],
        axis=0,
    )
    cross = dot6(proj[...], proj[...], TN)
    matrix = dot6(inverse, cross)
    polar = matrix / jnp.sqrt(jnp.sum(matrix * matrix, keepdims=True) + 1e-12)
    for _ in range(NS_STEPS):
        square = dot6(polar, polar, NT)
        mixed = coef_second * square + coef_third * dot6(square, square)
        polar = coef_first * polar + dot6(mixed, polar)
    m_buf[...] = dot6(inverse, polar, TN) * scale_out

    def share(o):
        return pltpu.make_async_remote_copy(
            src_ref=m_buf,
            dst_ref=m_in.at[o - 1],
            send_sem=m_send.at[o - 1],
            recv_sem=m_recv.at[o - 1],
            device_id={"dp": lax.rem(group + o, groups)},
            device_id_type=MESH,
        )

    for o in range(1, groups):
        share(o).start()
    own = halves(m_buf[...])

    @pl.loop(0, chunks)
    def _(c):
        o_ref[columns(c), :] = dot3(halves(pit[c].T), own)

    for o in range(1, groups):
        share(o).wait()
        theirs = halves(m_in[o - 1])

        @pl.loop(0, chunks)
        def _(c):
            exchange(c, o).wait()
            o_ref[columns(c), :] += dot3(halves(pit_in[o - 1, c].T), theirs)


def per_device(feature_slab, basis_start):
    feats, groups = lax.axis_size("feat"), lax.axis_size("dp")
    rows, features = feature_slab.shape
    rank = basis_start.shape[1]
    half = rank // 2
    width = 256 if features % 256 == 0 else features
    chunks = features // width
    stages = stages_of(feats)
    g_rows = -(-3 * half // (8 * feats)) * 8 * feats
    copies = sum(r - 1 for r, _ in stages)
    f32 = jnp.float32

    def slots(count, cols):
        out = []
        for radix, _ in stages:
            count //= radix
            out.append(pltpu.VMEM((radix - 1, count, cols), f32))
        return out

    scratch = [
        pltpu.VMEM((rows, rank), f32),
        pltpu.VMEM((rows, rank), f32),
        pltpu.VMEM((g_rows, half), f32),
        pltpu.VMEM((g_rows, half), f32),
        pltpu.VMEM((chunks, rank, width), f32),
        pltpu.VMEM((groups - 1, chunks, rank, width), f32),
        pltpu.VMEM((rank, rank), f32),
        pltpu.VMEM((groups - 1, rank, rank), f32),
        *slots(rows, rank),
        *slots(g_rows, half),
        *[pltpu.SemaphoreType.DMA((copies,)) for _ in range(8)],
        pltpu.SemaphoreType.DMA((groups - 1, chunks)),
        pltpu.SemaphoreType.DMA((groups - 1, chunks)),
        pltpu.SemaphoreType.DMA((groups - 1,)),
        pltpu.SemaphoreType.DMA((groups - 1,)),
    ]
    scale_out = math.sqrt(features * feats) / groups
    return pl.pallas_call(
        functools.partial(kernel, (stages, groups, chunks, width, scale_out)),
        out_shape=jax.ShapeDtypeStruct((features, rank), f32),
        in_specs=[pl.BlockSpec(memory_space=pltpu.VMEM)] * 2,
        out_specs=pl.BlockSpec(memory_space=pltpu.VMEM),
        scratch_shapes=scratch,
        compiler_params=pltpu.CompilerParams(
            collective_id=0, has_side_effects=True, vmem_limit_bytes=48 * 2**20
        ),
    )(feature_slab, basis_start)


def solution(mesh):
    placed = (P("dp", "feat"), P("feat", None))
    return jax.shard_map(
        per_device, mesh=mesh, in_specs=placed, out_specs=P("feat", None), check_vma=False
    )
```

time: 355 us -> 94.5 us (0.27)
  waiting for transfers between devices: 241 us -> 0 us
  Pallas kernels: 0 us -> 91.6 us
  other arithmetic: 57.9 us -> 0 us
  matrix products: 32.9 us -> 0 us
  between operations: 15.3 us -> 0.01 us
  local copies, waits for them, and re-layouts: 6.71 us -> 2.73 us
    psum x3 -> x0, waiting for transfers between devices: 241 us -> none  [the longest x1 92.9 us: per_device(): projected = lax.psum(plain_dot(feature_slab, basis), 'feat')]
    pallas_call x0 -> x1, Pallas kernels: none -> 91.6 us  [per_device(): pl.pallas_call(functools.partial(kernel, (stages, groups, chunks, width,...]
    another operation x9 -> x0, other arithmetic: 54 us -> none  [the longest x6 34 us: cholesky_inverse(): lower_factor = jnp.linalg.cholesky(gram_matrix)]
    dot_general x22 -> x0, matrix products: 31.6 us -> none  [the longest x19 21.4 us: plain_dot(): jnp.dot(left, right, precision=lax.Precision.HIGHEST, preferred_element_t...]
    another operation x9 -> x0, local copies, waits for them, and re-layouts: 4.12 us -> none
  transfers between devices with their start and end apart: 3 -> 0, of which waited for: 3 -> 0; matrix products, arithmetic and copies ran while one was open for 0% -> 0% of each run, Pallas kernels for 0% -> 0%
where the time goes in v1:
time: 94.5 us; the launch traced here: 94.4 us
  Pallas kernels  91.6 us (97%)
  local copies, waits for them, and re-layouts  2.73 us (3%)
    pallas_call x1, Pallas kernels, per_device(): pl.pallas_call(functools.partial(kernel, (stages, groups, chunks, width,...  91.6 us
    unnamed x3, local copies, waits for them, and re-layouts  2.73 us

profile of v1, /device:TPU:0, one launch (start us, length us, event | category | flops | bytes accessed | tf_op | source)
XLA Modules:
  0.0 94.4 jit_solution(11799130027454823759)
XLA Ops:
  0.0 0.0 copy-start
  0.0 1.5 %copy-done = f32[1792,256]{1,0:T(8,128)S(1)} copy-done((f32[1792,256]{1,0:T(8,128)S(1)}, f32[1792,256]{1,0:T(8,128)}, u32[]{:S(2)}) %copy-start) | copy-done | bytes 1835032
  1.5 91.6 %shard_map.28 = f32[1792,256]{1,0:T(8,128)S(1)} custom-call(f32[512,1792]{1,0:T(8,128)} %a_ref.1, f32[1792,256]{1,0:T(8,128)S(1)} %copy-done), custom_call_target="tpu_custom_call" | custom-call | tf_op jit(solution)/shard_map/pallas_call | solution.py:295
  93.1 1.2 %copy.4 = f32[1792,256]{1,0:T(8,128)} copy(f32[1792,256]{1,0:T(8,128)S(1)} %shard_map.28) | data formatting | bytes 3670016
Async XLA Ops:
  0.0 1.5 %copy-start = (f32[1792,256]{1,0:T(8,128)S(1)}, f32[1792,256]{1,0:T(8,128)}, u32[]{:S(2)}) copy-start(f32[1792,256]{1,0:T(8,128)} %b_ref.1) | copy-start | bytes 5505028
